TPU v7x, 32 devices: a whole 2x2x4 slice. The times are simulated.
32 devices in a mesh: dp: 16 (over z, x, core), mp: 2 (over y).
Axes of the slice: x: 2, y: 2, z: 4, core: 2. Of those that a mesh axis runs over, the one named last changes fastest.
Arguments:
- inputs: bfloat16 [32, 3072, 512], P(('dp', 'mp')), may hold values from -6 to 6
- crop_ids: int32 [32, 3072], P('dp'), may hold values from 0 to 3, as said below
- w_heads: bfloat16 [512, 3, 512], P(None, None, 'mp'), may hold values from -0.25 to 0.25
- b_heads: float32 [2, 512], P(None, 'mp'), may hold values from -3 to 3
- w_merge: bfloat16 [512, 512], P('mp'), may hold values from -2 to 2
- b_merge: float32 [512], replicated, may hold values from -3 to 3
- gain_one: float32 [512], replicated, may hold values from 0.5 to 1.5
- shift_one: float32 [512], replicated, may hold values from -2 to 2
- w_expand: bfloat16 [512, 2048], P(None, 'mp'), may hold values from -0.25 to 0.25
- b_expand: float32 [2048], P('mp'), may hold values from -3 to 3
- w_reduce: bfloat16 [2048, 512], P('mp'), may hold values from -0.125 to 0.125
- b_reduce: float32 [512], replicated, may hold values from -3 to 3
- gain_two: float32 [512], replicated, may hold values from 0.5 to 1.5
- shift_two: float32 [512], replicated, may hold values from -2 to 2
- cotangent: bfloat16 [32, 3072, 512], P(('dp', 'mp')), may hold values from -6 to 6
Outputs:
- outputs: bfloat16 [32, 3072, 512], P(('dp', 'mp'))
- grad_inputs: float32 [32, 3072, 512], P(('dp', 'mp'))
- grad_w_heads: float32 [512, 3, 512], P(None, None, 'mp')
- grad_b_heads: float32 [2, 512], P(None, 'mp')
- grad_w_merge: float32 [512, 512], P('mp')
- grad_b_merge: float32 [512], replicated
- grad_gain_one: float32 [512], replicated
- grad_shift_one: float32 [512], replicated
- grad_w_expand: float32 [512, 2048], P(None, 'mp')
- grad_b_expand: float32 [2048], P('mp')
- grad_w_reduce: float32 [2048, 512], P('mp')
- grad_b_reduce: float32 [512], replicated
- grad_gain_two: float32 [512], replicated
- grad_shift_two: float32 [512], replicated
Inputs may be any that keep to these rules, and one draw needn't show every extreme that they name: `crop_ids`: along a canvas's raster order its crop ids never fall; a canvas holds at most four crops.
All inputs are finite; a program needn't handle non-finite values.
Results may differ from a plain program's by a relative error of at most 0.028.
Values may be sent and summed in bfloat16 or wider, within the bound.
A program may use at most 320 MiB of HBM per device.

v0:
```python
import math

import jax
import jax.numpy as jnp
import numpy as np
from jax import lax
from jax.sharding import PartitionSpec as P

HD = 64
CROWS = 32
CCOLS = 96
QROWS = 8
QCOLS = 32
POS = 3072


def geometry():
    across = CCOLS // QCOLS
    blocks = CROWS // QROWS * across
    order = np.arange(blocks)
    block_row = order // across * QROWS
    block_col = order % across * QCOLS
    query_at = np.arange(QROWS * QCOLS)
    query_row = block_row[:, None] + query_at[None, :] // QCOLS
    query_col = block_col[:, None] + query_at[None, :] % QCOLS
    key_at = np.arange(4 * QROWS * QCOLS)
    key_row = block_row[:, None] + key_at[None, :] // (2 * QCOLS) - QROWS
    key_col = block_col[:, None] + key_at[None, :] % (2 * QCOLS) - QCOLS // 2
    earlier = key_row[:, None, :] < query_row[:, :, None]
    level = (key_row[:, None, :] == query_row[:, :, None]) & (
        key_col[:, None, :] <= query_col[:, :, None]
    )
    return jnp.asarray(earlier | level)


def to_blocks(tensor):
    trailing = tensor.shape[1:]
    canvas_grid = tensor.reshape((CROWS // QROWS, QROWS, CCOLS // QCOLS, QCOLS) + trailing)
    canvas_grid = jnp.swapaxes(canvas_grid, 1, 2)
    return canvas_grid.reshape((CROWS // QROWS * (CCOLS // QCOLS), QROWS * QCOLS) + trailing)


def from_blocks(tensor):
    trailing = tensor.shape[2:]
    canvas_grid = tensor.reshape((CROWS // QROWS, CCOLS // QCOLS, QROWS, QCOLS) + trailing)
    canvas_grid = jnp.swapaxes(canvas_grid, 1, 2)
    return canvas_grid.reshape((POS,) + trailing)


def memory(tensor, filler):
    trailing = tensor.shape[1:]
    canvas_grid = tensor.reshape((CROWS, CCOLS) + trailing)
    widths = ((QROWS, 0), (QCOLS // 2, QCOLS // 2)) + ((0, 0),) * len(trailing)
    canvas_grid = jnp.pad(canvas_grid, widths, constant_values=filler)
    across = CCOLS // QCOLS
    pieces = []
    for number in range(CROWS // QROWS * across):
        row_at = number // across * QROWS
        col_at = number % across * QCOLS
        portion = canvas_grid[row_at : row_at + 2 * QROWS, col_at : col_at + 2 * QCOLS]
        pieces.append(portion.reshape((4 * QROWS * QCOLS,) + trailing))
    return jnp.stack(pieces)


def unmemory(stacked):
    trailing = stacked.shape[2:]
    canvas_grid = jnp.zeros((CROWS + QROWS, CCOLS + QCOLS) + trailing, stacked.dtype)
    across = CCOLS // QCOLS
    for number in range(stacked.shape[0]):
        row_at = number // across * QROWS
        col_at = number % across * QCOLS
        portion = stacked[number].reshape((2 * QROWS, 2 * QCOLS) + trailing)
        canvas_grid = canvas_grid.at[row_at : row_at + 2 * QROWS, col_at : col_at + 2 * QCOLS].add(
            portion
        )
    return canvas_grid[QROWS:, QCOLS // 2 : QCOLS // 2 + CCOLS].reshape((POS,) + trailing)


def allowed_pairs(labels):
    matching = to_blocks(labels)[:, :, None] == memory(labels, -1)[:, None, :]
    return geometry() & matching


def split_heads(packed):
    head_width = packed.shape[1] // 3
    head_count = head_width // HD
    query_blocks = to_blocks(packed[:, :head_width].reshape(POS, head_count, HD))
    key_blocks = memory(packed[:, head_width : 2 * head_width].reshape(POS, head_count, HD), 0)
    value_blocks = memory(packed[:, 2 * head_width :].reshape(POS, head_count, HD), 0)
    return (query_blocks, key_blocks, value_blocks)


def attend_forward(packed, labels):
    head_width = packed.shape[1] // 3
    scaling = 1.0 / math.sqrt(HD)
    query_blocks, key_blocks, value_blocks = split_heads(packed)
    scores = (
        jnp.einsum("bqhe,bkhe->bhqk", query_blocks, key_blocks, preferred_element_type=jnp.float32)
        * scaling
    )
    masked = jnp.where(allowed_pairs(labels)[:, None], scores, -1000000000.0)
    maximum = jnp.max(masked, axis=-1, keepdims=True)
    exponent = jnp.exp(masked - maximum)
    totals = jnp.sum(exponent, axis=-1, keepdims=True)
    rounded = (exponent / totals).astype(jnp.bfloat16)
    combined = jnp.einsum(
        "bhqk,bkhe->bqhe", rounded, value_blocks, preferred_element_type=jnp.float32
    )
    return (from_blocks(combined).reshape(POS, head_width).astype(jnp.bfloat16), maximum, totals)


def attend_backward(packed, grad_combined, labels, maximum, totals):
    head_width = packed.shape[1] // 3
    head_count = head_width // HD
    scaling = 1.0 / math.sqrt(HD)
    query_blocks, key_blocks, value_blocks = split_heads(packed)
    scores = (
        jnp.einsum("bqhe,bkhe->bhqk", query_blocks, key_blocks, preferred_element_type=jnp.float32)
        * scaling
    )
    masked = jnp.where(allowed_pairs(labels)[:, None], scores, -1000000000.0)
    chances = jnp.exp(masked - maximum) / totals
    rounded = chances.astype(jnp.bfloat16)
    grad_blocks = to_blocks(grad_combined.reshape(POS, head_count, HD))
    grad_chances = jnp.einsum(
        "bqhe,bkhe->bhqk", grad_blocks, value_blocks, preferred_element_type=jnp.float32
    )
    grad_scores = (
        chances * (grad_chances - jnp.sum(grad_chances * chances, axis=-1, keepdims=True))
    ).astype(jnp.bfloat16)
    grad_queries = (
        jnp.einsum("bhqk,bkhe->bqhe", grad_scores, key_blocks, preferred_element_type=jnp.float32)
        * scaling
    )
    grad_keys = (
        jnp.einsum("bhqk,bqhe->bkhe", grad_scores, query_blocks, preferred_element_type=jnp.float32)
        * scaling
    )
    grad_values = jnp.einsum(
        "bhqk,bqhe->bkhe", rounded, grad_blocks, preferred_element_type=jnp.float32
    )
    grad_queries = from_blocks(grad_queries).reshape(POS, head_width)
    grad_keys = unmemory(grad_keys).reshape(POS, head_width)
    grad_values = unmemory(grad_values).reshape(POS, head_width)
    return jnp.concatenate([grad_queries, grad_keys, grad_values], axis=1).astype(jnp.bfloat16)


def regroup(packed, groups):
    parted = packed.reshape(POS, 3, groups, packed.shape[1] // (3 * groups))
    return jnp.transpose(parted, (2, 0, 1, 3)).reshape(groups, POS, packed.shape[1] // groups)


def ungroup(grouped):
    return jnp.transpose(grouped, (1, 0, 2)).reshape(POS, grouped.shape[0] * grouped.shape[2])


def ungroup_packed(grouped):
    groups = grouped.shape[0]
    width = grouped.shape[2] // 3
    parted = grouped.reshape(groups, POS, 3, width)
    return jnp.transpose(parted, (1, 2, 0, 3)).reshape(POS, 3 * groups * width)


def normalize(tensor, gain_vec, shift_vec):
    centered = tensor - jnp.mean(tensor, axis=-1, keepdims=True)
    variance = jnp.mean(centered * centered, axis=-1, keepdims=True)
    return centered * lax.rsqrt(variance + 1e-05) * gain_vec + shift_vec


def smooth_gelu(tensor):
    return (
        0.5
        * tensor
        * (1.0 + jnp.tanh(0.7978845608028654 * (tensor + 0.044715 * tensor * tensor * tensor)))
    )


def local(
    inputs,
    crop_ids,
    w_heads,
    b_heads,
    w_merge,
    b_merge,
    gain_one,
    shift_one,
    w_expand,
    b_expand,
    w_reduce,
    b_reduce,
    gain_two,
    shift_two,
    cotangent,
):
    own_count = inputs.shape[0]
    features = w_heads.shape[0]
    own_labels = lax.dynamic_slice_in_dim(crop_ids, lax.axis_index("mp") * own_count, own_count, 0)
    full_heads, full_bias, full_merge, full_expand, full_bexp, full_reduce = (
        lax.all_gather(w_heads, "mp", axis=2, tiled=True),
        lax.all_gather(b_heads.astype(jnp.bfloat16), "mp", axis=1, tiled=True).astype(
            b_heads.dtype
        ),
        lax.all_gather(w_merge, "mp", axis=0, tiled=True),
        lax.all_gather(w_expand, "mp", axis=1, tiled=True),
        lax.all_gather(b_expand.astype(jnp.bfloat16), "mp", axis=0, tiled=True).astype(
            b_expand.dtype
        ),
        lax.all_gather(w_reduce, "mp", axis=0, tiled=True),
    )
    width_all = full_heads.shape[2]
    groups = width_all // (2 * HD)
    heads_all = full_heads.reshape(features, 3 * width_all)
    bias_all = jnp.concatenate([full_bias[0], jnp.zeros_like(full_bias[0]), full_bias[1]])
    packed = (
        jnp.einsum("cpd,dk->cpk", inputs, heads_all, preferred_element_type=jnp.float32) + bias_all
    ).astype(jnp.bfloat16)

    def forward_canvas(bundle):
        canvas_packed, labels = bundle

        def forward_group(group_packed):
            return attend_forward(group_packed, labels)

        group_out, group_max, group_tot = lax.map(forward_group, regroup(canvas_packed, groups))
        return (ungroup(group_out), group_max, group_tot)

    attended, maxima, totals = lax.map(forward_canvas, (packed, own_labels))
    branch_one = jnp.einsum("cpk,kd->cpd", attended, full_merge, preferred_element_type=jnp.float32)
    summed_one = inputs.astype(jnp.float32) + branch_one + b_merge
    normed_one, norm_one_back = jax.vjp(normalize, summed_one, gain_one, shift_one)
    expanded_in = normed_one.astype(jnp.bfloat16)
    hidden_pre = (
        jnp.einsum("cpd,df->cpf", expanded_in, full_expand, preferred_element_type=jnp.float32)
        + full_bexp
    )
    hidden_act, gelu_back = jax.vjp(smooth_gelu, hidden_pre)
    hidden = hidden_act.astype(jnp.bfloat16)
    branch_two = jnp.einsum("cpf,fd->cpd", hidden, full_reduce, preferred_element_type=jnp.float32)
    summed_two = normed_one + branch_two + b_reduce
    result, norm_two_back = jax.vjp(normalize, summed_two, gain_two, shift_two)
    outputs = result.astype(jnp.bfloat16)
    grad_two, grad_gain_two, grad_shift_two = norm_two_back(cotangent.astype(jnp.float32))
    grad_b_reduce = jnp.sum(grad_two, axis=(0, 1))
    grad_rows = grad_two.astype(jnp.bfloat16)
    local_w_reduce = jnp.einsum(
        "cpf,cpd->fd", hidden, grad_rows, preferred_element_type=jnp.float32
    )
    grad_hidden = jnp.einsum(
        "cpd,fd->cpf", grad_rows, full_reduce, preferred_element_type=jnp.float32
    )
    grad_pre = gelu_back(grad_hidden)[0].astype(jnp.bfloat16)
    local_b_expand = jnp.sum(grad_pre, axis=(0, 1), dtype=jnp.float32)
    local_w_expand = jnp.einsum(
        "cpd,cpf->df", expanded_in, grad_pre, preferred_element_type=jnp.float32
    )
    grad_normed = grad_two + jnp.einsum(
        "cpf,df->cpd", grad_pre, full_expand, preferred_element_type=jnp.float32
    )
    grad_one, grad_gain_one, grad_shift_one = norm_one_back(grad_normed)
    grad_b_merge = jnp.sum(grad_one, axis=(0, 1))
    grad_attn_rows = grad_one.astype(jnp.bfloat16)
    local_w_merge = jnp.einsum(
        "cpk,cpd->kd", attended, grad_attn_rows, preferred_element_type=jnp.float32
    )
    grad_attended = jnp.einsum(
        "cpd,kd->cpk", grad_attn_rows, full_merge, preferred_element_type=jnp.float32
    ).astype(jnp.bfloat16)

    def backward_canvas(bundle):
        canvas_packed, canvas_grad, labels, canvas_max, canvas_tot = bundle
        grad_groups = jnp.transpose(
            canvas_grad.reshape(POS, groups, width_all // groups), (1, 0, 2)
        )

        def backward_group(parts):
            return attend_backward(parts[0], parts[1], labels, parts[2], parts[3])

        return ungroup_packed(
            lax.map(
                backward_group,
                (regroup(canvas_packed, groups), grad_groups, canvas_max, canvas_tot),
            )
        )

    grad_packed = lax.map(backward_canvas, (packed, grad_attended, own_labels, maxima, totals))
    grad_bias_all = jnp.sum(grad_packed, axis=(0, 1), dtype=jnp.float32)
    local_b_heads = jnp.stack([grad_bias_all[:width_all], grad_bias_all[2 * width_all :]])
    local_w_heads = jnp.einsum(
        "cpd,cpk->dk", inputs, grad_packed, preferred_element_type=jnp.float32
    ).reshape(features, 3, width_all)
    grad_inputs = grad_one + jnp.einsum(
        "cpk,dk->cpd", grad_packed, heads_all, preferred_element_type=jnp.float32
    )
    grad_w_heads, grad_b_heads, grad_w_merge, grad_w_expand, grad_b_expand, grad_w_reduce = (
        lax.psum_scatter(
            local_w_heads.astype(jnp.bfloat16), "mp", scatter_dimension=2, tiled=True
        ).astype(jnp.float32),
        lax.psum_scatter(
            local_b_heads.astype(jnp.bfloat16), "mp", scatter_dimension=1, tiled=True
        ).astype(jnp.float32),
        lax.psum_scatter(
            local_w_merge.astype(jnp.bfloat16), "mp", scatter_dimension=0, tiled=True
        ).astype(jnp.float32),
        lax.psum_scatter(
            local_w_expand.astype(jnp.bfloat16), "mp", scatter_dimension=1, tiled=True
        ).astype(jnp.float32),
        lax.psum_scatter(
            local_b_expand.astype(jnp.bfloat16), "mp", scatter_dimension=0, tiled=True
        ).astype(jnp.float32),
        lax.psum_scatter(
            local_w_reduce.astype(jnp.bfloat16), "mp", scatter_dimension=0, tiled=True
        ).astype(jnp.float32),
    )
    grad_w_expand, grad_b_expand, grad_w_reduce = (
        lax.psum(grad_w_expand.astype(jnp.bfloat16), "dp").astype(jnp.float32),
        lax.psum(grad_b_expand.astype(jnp.bfloat16), "dp").astype(jnp.float32),
        lax.psum(grad_w_reduce.astype(jnp.bfloat16), "dp").astype(jnp.float32),
    )
    grad_w_heads, grad_b_heads, grad_w_merge = (
        lax.psum(grad_w_heads.astype(jnp.bfloat16), "dp").astype(jnp.float32),
        lax.psum(grad_b_heads.astype(jnp.bfloat16), "dp").astype(jnp.float32),
        lax.psum(grad_w_merge.astype(jnp.bfloat16), "dp").astype(jnp.float32),
    )
    grad_b_merge, grad_gain_one, grad_shift_one, grad_b_reduce, grad_gain_two, grad_shift_two = (
        lax.psum(
            (
                grad_b_merge,
                grad_gain_one,
                grad_shift_one,
                grad_b_reduce,
                grad_gain_two,
                grad_shift_two,
            ),
            ("dp", "mp"),
        )
    )
    return (
        outputs,
        grad_inputs,
        grad_w_heads,
        grad_b_heads,
        grad_w_merge,
        grad_b_merge,
        grad_gain_one,
        grad_shift_one,
        grad_w_expand,
        grad_b_expand,
        grad_w_reduce,
        grad_b_reduce,
        grad_gain_two,
        grad_shift_two,
    )


def solution(mesh):
    return jax.shard_map(
        local,
        mesh=mesh,
        in_specs=(
            P(("dp", "mp"), None, None),
            P("dp", None),
            P(None, None, "mp"),
            P(None, "mp"),
            P("mp", None),
            P(),
            P(),
            P(),
            P(None, "mp"),
            P("mp"),
            P("mp", None),
            P(),
            P(),
            P(),
            P(("dp", "mp"), None, None),
        ),
        out_specs=(
            P(("dp", "mp"), None, None),
            P(("dp", "mp"), None, None),
            P(None, None, "mp"),
            P(None, "mp"),
            P("mp", None),
            P(),
            P(),
            P(),
            P(None, "mp"),
            P("mp"),
            P("mp", None),
            P(),
            P(),
            P(),
        ),
        check_vma=False,
    )
```

profile of v0, /device:TPU:0, one launch (start us, length us, event | category | flops | bytes accessed | tf_op | source)
XLA Modules:
  0.0 5456.8 jit_solution(10359668127216779538)
XLA Ops:
  63.1 537.9 %while.73 = (s32[]{:T(128)}, bf16[4,3072,128]{1,2,0:T(8,128)(2,1)}, f32[4,12,2,256,1]{3,2,1,4,0:T(2,128)}, f32[4,12,2,256,1]{3,2,1,4,0:T(2,128)}, bf16[4,3072,38...) while((s32[]{:T(128)}, bf16[4,3072,128]{1,2,0:T(8,128)(2,1)}, ...), condition=%wide.region_3.4_spmd.clone, body=%wide.region_0.3_spmd.sunk.clone.sunk | while | flops 1692782592 | bytes 198324656 | solution.py:224
  724.6 4483.7 %while.74 = (s32[]{:T(128)}, bf16[4,3072,384]{1,2,0:T(8,128)(2,1)}, bf16[4,3072,384]{1,2,0:T(8,128)(2,1)}, s32[3072]{0:T(1024)S(1)}, f32[4,12,2,256,1]{3,2,1,4,0...) while((s32[]{:T(128)}, bf16[4,3072,384]{1,2,0:T(8,128)(2,1)}, ...), condition=%wide.region_16.17_spmd.clone, body=%wide.region_12.16_spmd.sunk.clone.sunk | while | flops 4108576768 | bytes 526816736 | solution.py:279
  861.2 48.1 scatter-add.199
  913.8 48.0 scatter-add.200
  979.2 46.7 scatter-add.202
  1028.5 47.2 scatter-add.203
  1390.8 48.1 scatter-add.211
  1443.4 48.0 scatter-add.212
  1508.8 46.7 scatter-add.214
  1558.1 46.7 scatter-add.215
  1622.2 47.1 scatter-add.217
  1980.1 48.1 scatter-add.199
  2032.7 48.0 scatter-add.200
  2098.1 46.7 scatter-add.202
  2147.4 46.9 scatter-add.203
  2509.7 48.1 scatter-add.211
  2562.2 48.0 scatter-add.212
  2677.0 46.7 scatter-add.215
  2741.1 46.9 scatter-add.217
  3098.8 48.1 scatter-add.199
  3151.3 48.0 scatter-add.200
  3266.0 47.2 scatter-add.203
  3628.4 48.1 scatter-add.211
  3680.9 48.0 scatter-add.212
  3859.7 47.1 scatter-add.217
  4217.7 48.1 scatter-add.199
  4270.3 48.0 scatter-add.200
  4335.7 46.7 scatter-add.202
  4385.0 46.9 scatter-add.203
  4747.3 48.1 scatter-add.211
  4799.8 48.0 scatter-add.212
  4978.7 46.9 scatter-add.217
  (1579 shorter events, 3985.0 us)
Async XLA Ops:
  7.2 36.3 copy-start
  7.2 28.4 copy-start.56
  7.2 38.0 all-gather.4.cloned.1.call-start
  9.8 599.3 %all-gather.6.cloned.1.call-start = ((), (), s32[]{:S(2)}) async-start(), calls=%async_computation.6 | async-start | bytes 3145728 | tf_op jit(solution)/shard_map/all_gather | solution.py:204
  10.5 621.3 %all-gather.8.cloned.1.call-start = ((), (), s32[]{:S(2)}) async-start(), calls=%async_computation.7 | async-start | bytes 3145728 | tf_op jit(solution)/shard_map/all_gather | solution.py:208
  11.2 5248.6 %reduce-scatter.10.cloned.1.call-start = ((), (), s32[]{:S(2)}) async-start(), calls=%async_computation.9 | async-start | bytes 786432 | tf_op jit(solution)/shard_map/reduce_scatter | solution.py:301
  63.1 537.9 %copy-start.89 = (f32[512]{0:T(512)S(1)}, f32[512]{0:T(512)}, u32[]{:S(2)}) copy-start(f32[512]{0:T(512)} %param.74) | copy-start | bytes 6148
  100.5 17.2 copy-start.33
  606.4 101.4 %copy-start.63 = (f32[3072]{0:T(1024)}, f32[3072]{0:T(1024)S(1)}, u32[]{:S(2)}) copy-start(f32[3072]{0:T(1024)S(1)} %broadcast_multiply_fusion.1) | copy-start | bytes 36868
  609.1 98.7 %copy-start.69 = (f32[3072]{0:T(1024)}, f32[3072]{0:T(1024)S(1)}, u32[]{:S(2)}) copy-start(f32[3072]{0:T(1024)S(1)} %fusion.43) | copy-start | bytes 36868
  609.1 22.8 copy-start.90
  631.8 20.1 copy-start.40
  656.2 37.8 slice-start
  660.6 33.4 copy-start.49
  660.6 33.4 copy-start.65
  660.6 33.4 slice-start.1
  660.6 33.4 copy-start.86
  721.7 4538.1 %reduce-scatter.8.cloned.1.call-start = ((), (), s32[]{:S(2)}) async-start(), calls=%async_computation.8 | async-start | bytes 2359296 | tf_op jit(solution)/shard_map/reduce_scatter | solution.py:295
  753.5 17.2 copy-start.34
  1323.9 21.3 copy-start.9
  1872.2 17.2 copy-start.34
  2442.6 21.3 copy-start.9
  2991.1 17.2 copy-start.34
  3561.4 21.3 copy-start.9
  4109.8 17.2 copy-start.34
  4680.2 21.3 copy-start.9
  5225.7 61.4 %reduce-scatter.14.cloned.1.call-start = ((), (), s32[]{:S(2)}) async-start(), calls=%async_computation.11 | async-start | bytes 3145728 | tf_op jit(solution)/shard_map/reduce_scatter | solution.py:310
  5239.8 82.1 %reduce-scatter.12.cloned.1.call-start = ((), (), s32[]{:S(2)}) async-start(), calls=%async_computation.10 | async-start | bytes 3145728 | tf_op jit(solution)/shard_map/reduce_scatter | solution.py:304
  5252.6 142.6 %reduce-scatter.16.cloned.1.call-start = ((), (), s32[]{:S(2)}) async-start(), calls=%async_computation.12 | async-start | bytes 196608
  5257.6 64.3 %copy-start.68 = (f32[3072]{0:T(1024)S(1)}, f32[3072]{0:T(1024)}, u32[]{:S(2)}) copy-start(f32[3072]{0:T(1024)} %copy-done.67) | copy-start | bytes 36868
  5257.6 64.3 %copy-start.88 = (bf16[512,3,512]{0,2,1:T(8,128)(2,1)S(1)}, bf16[512,3,512]{0,2,1:T(8,128)(2,1)}, u32[]{:S(2)}) copy-start(bf16[512,3,512]{0,2,1:T(8,128)(2,1)} %all-gather.4.cloned.1.call-done) | copy-start | bytes 4718596
  5258.5 183.9 %all-reduce.14.cloned.1.call-start = ((), (), s32[]{:S(2)}) async-start(), calls=%async_computation.13 | async-start | bytes 6291456 | tf_op jit(solution)/shard_map/psum | solution.py:320
  (217 other events, 1695.1 us)
Sparse Core Ops, SparseCore 0:
  10.2 35.0 all-gather.3
  46.8 33.6 all-gather.5
  82.0 33.1 all-gather.7
  721.8 15.3 reduce-scatter.9
  5225.7 26.7 reduce-scatter.7
  5255.3 31.8 reduce-scatter.13
  5290.0 31.8 reduce-scatter.11
  5324.1 10.2 reduce-scatter.15
  5338.3 104.0 all-reduce.13
where the time goes:
time: 5470 us; the launch traced here: 5460 us
  local copies, waits for them, and re-layouts  4280 us (78%)
  matrix products  488 us (9%)
  other arithmetic  463 us (8%)
  blocking collectives  101 us (2%)
  waiting for transfers between devices  77.5 us (1%)
    scatter-add x96, local copies, waits for them, and re-layouts, unmemory(): canvas_grid.at[row_at:row_at + 2 * QROWS, col_at:col_at + 2 * QCOLS]  3320 us
    reshape x288, local copies, waits for them, and re-layouts, memory(): return jnp.stack(pieces)  292 us
    add x72, other arithmetic, unmemory(): canvas_grid.at[row_at:row_at + 2 * QROWS, col_at:col_at + 2 * QCOLS]  179 us
    while x560, local copies, waits for them, and re-layouts  175 us
    another operation x96, local copies, waits for them, and re-layouts  127 us
  transfers between devices with their start and end apart: 9, of which 4 were waited for; matrix products, arithmetic and copies ran while one was open for 94% of the time, Pallas kernels for 0%

commit v1 on v0

v1 whole, which is shorter than its diff:
```python
import functools

import jax
import jax.numpy as jnp
from jax import lax
from jax.experimental import pallas as pl
from jax.experimental.pallas import tpu as pltpu
from jax.sharding import PartitionSpec as P

D = 512
FF = 2048
HD = 64
CROWS = 32
CCOLS = 96
QROWS = 8
QCOLS = 32
POS = 3072
QB = QROWS * QCOLS
PAIR = 2 * HD
BIG = 1e30
LOG2E = 1.4426950408889634
HALF = QROWS // 2
LATE = 2 * HALF * QCOLS
AT_EARLY = (0, 12 * 48, 12 * (48 + 64))
AT_LATE = (0, 16 * 48, 16 * (48 + 64))
ROWS_EARLY, ROWS_LATE = 12 * 160, 16 * 160
MIB = 1 << 20
COLS = ((0, 0, 48), (32, 16, 64), (64, 48, 48))
GC = 0.7978845608028654
GA = 0.044715

f32 = jnp.float32
bf16 = jnp.bfloat16


def dot(a, b):
    return lax.dot_general(a, b, (((1,), (0,)), ((), ())), preferred_element_type=f32)


def dot_nt(a, b):
    return lax.dot_general(a, b, (((1,), (1,)), ((), ())), preferred_element_type=f32)


def dot_tn(a, b):
    return lax.dot_general(a, b, (((0,), (0,)), ((), ())), preferred_element_type=f32)


def sliced(function, step, *arrays):
    results = [
        function(*(array[at : at + step] for array in arrays)) for at in range(0, arrays[0].shape[0], step)
    ]
    if isinstance(results[0], tuple):
        return tuple(jnp.concatenate(parts, axis=0) for parts in zip(*results))
    return jnp.concatenate(results, axis=0)


def lanes_of(value):
    return lax.broadcasted_iota(jnp.int32, value.shape, value.ndim - 1)


def lane_row(first, count, scale=1.0):
    lane = lax.broadcasted_iota(jnp.int32, (1, PAIR), 1)
    return jnp.where((lane >= first) & (lane < first + count), scale, 0.0).astype(bf16)


def own_lanes(value, head, scale=1.0):
    return value * lane_row(head * HD, HD, scale)


def stacked(first, second):
    half = first.shape[0] // 2
    return jnp.concatenate([first[:half], second[:half], first[half:], second[half:]], axis=0)


def key_rows(i):
    if isinstance(i, int):
        return slice(max(i - 1, 0) * QROWS, (i + 1) * QROWS)
    return pl.ds(pl.multiple_of(i * QROWS - QROWS, QROWS), 2 * QROWS)


def query_rows(i):
    return pl.ds(i * QROWS if isinstance(i, int) else pl.multiple_of(i * QROWS, QROWS), QROWS)


def window(ref, i, c0, width):
    keys = ref[key_rows(i), c0 : c0 + width, :]
    return keys.reshape(keys.shape[0] * width, keys.shape[2])


def put_tiles(ref, at, value):
    for k in range(value.shape[1] // PAIR):
        ref[k, at : at + value.shape[0], :] = value[:, k * PAIR : (k + 1) * PAIR]


def get_tiles(ref, at, size):
    return jnp.concatenate([ref[k, at : at + size, :] for k in range(ref.shape[0])], axis=1)


def powers(scores, top):
    return jnp.exp2(((scores - top) * LOG2E).astype(bf16))


def three_parts(value):
    parts = []
    for _ in range(3):
        parts.append(value.astype(bf16).astype(f32))
        value = value - parts[-1]
    return parts


class Weights:
    def __init__(self, sources, targets, send, recv):
        self.sources, self.targets, self.send, self.recv = sources, targets, send, recv
        self.me, self.place = lax.axis_index("dp"), lax.axis_index("mp")
        self.core = lax.rem(self.me, 2)

    def copy(self, source, target, number, to):
        return pltpu.make_async_remote_copy(
            src_ref=source,
            dst_ref=target,
            send_sem=self.send.at[number],
            recv_sem=self.recv.at[number],
            device_id=to,
            device_id_type=pl.DeviceIdType.MESH,
        )

    def meet(self):
        barrier = pltpu.get_barrier_semaphore()
        for to in (self.across(), self.beside()):
            pl.semaphore_signal(barrier, inc=1, device_id=to, device_id_type=pl.DeviceIdType.MESH)
        pl.semaphore_wait(barrier, 2)

    def across(self):
        return self.me, 1 - self.place

    def beside(self):
        return self.me + 1 - 2 * self.core, self.place

    def half(self, ref):
        axis = len(ref.shape) - 2
        size = ref.shape[axis] // 2
        rows = pl.ds(pl.multiple_of(self.core * size, 8), size)
        return ref.at[(slice(None),) * axis + (rows,)]

    def first(self, name):
        source, target = self.sources[name], self.targets[name]
        if name < HEADS:
            return self.copy(source, target, 2 * name, self.across())
        return self.copy(self.half(source), self.half(target), 2 * name, self.across())

    def second(self, name):
        mine = self.half(self.targets[name])
        return self.copy(mine, mine, 2 * name + 1, self.beside())


QV, HIDDEN, HEADS, MERGE, EXPAND, REDUCE = range(6)


def attend_forward_kernel(talks, x_refs, w_ref, qv_ref, hot_ref, others, *refs):
    qkv_ref, att_ref, rate_ref, early_hbm, late_hbm, got = refs[:6]
    bias_ref, w_now, v_now, early_ref, late_ref, *ready_refs, sems, landing, talk = refs[6:]
    pair = pl.program_id(0)
    pairs = pl.num_programs(0)
    if talks:
        weights = Weights([qv_ref, others[0], w_ref, *others[1:]], [*landing, *got[HEADS + 1 :]], *talk)
        w_other, v_other = landing[HEADS], landing[QV]
    else:
        w_other, v_other = others

    @pl.when(pair == 0)
    def _():
        if talks:
            weights.meet()
            for name in (HEADS, QV, HIDDEN):
                weights.first(name).start()
        shape = (HALF, 2 * QCOLS, LATE)
        key_row = lax.broadcasted_iota(jnp.int32, shape, 0)
        key_col = lax.broadcasted_iota(jnp.int32, shape, 1) - QCOLS // 2
        query = lax.broadcasted_iota(jnp.int32, shape, 2) % (HALF * QCOLS)
        row, column = query // QCOLS, query % QCOLS
        later = (key_row > row) | ((key_row == row) & (key_col > column))
        bias_ref[...] = jnp.where(later, -BIG, 0.0).astype(f32)
        w_now[...] = w_ref[...]
        v_now[...] = qv_ref[...]

    @pl.when(pair == 2)
    def _():
        w_now[...] = w_other[...]
        v_now[...] = v_other[...]

    @pl.when(lax.rem(pair, 2) == 0)
    def _():
        spans = [slice(p * PAIR, (p + 1) * PAIR) for p in range(2)]
        full = jnp.concatenate([w_now[k][:, span] for span in spans for k in range(3)], axis=1)
        none = jnp.zeros((1, PAIR), f32)
        biases = jnp.concatenate(
            [part for span in spans for part in (v_now[0:1, span], none, v_now[1:2, span])], axis=1
        )

        @pl.loop(0, CROWS // 8)
        def _(step):
            rows = pl.ds(pl.multiple_of(step * 8, 8), 8)
            part = jnp.concatenate([ref[rows].reshape(8 * CCOLS, PAIR) for ref in x_refs], axis=1)
            qkv = (dot(part, full) + biases).astype(bf16)
            for k in range(6):
                qkv_ref[k // 3, k % 3, rows] = qkv[:, k * PAIR : (k + 1) * PAIR].reshape(8, CCOLS, PAIR)

    queries_ref, keys_ref, values_ref = (qkv_ref.at[lax.rem(pair, 2), part] for part in range(3))

    def copies(half):
        rows = pl.ds(2 * half, 2)
        return [
            pltpu.make_async_copy(early_ref.at[half], early_hbm.at[pair, rows], sems.at[half, 0]),
            pltpu.make_async_copy(late_ref.at[half], late_hbm.at[pair, rows], sems.at[half, 1]),
        ]

    def score(i, j):
        q0, c0, width = COLS[j]
        q_rows = query_rows(i)
        queries = queries_ref[q_rows, q0 : q0 + QCOLS, :].reshape(QB, PAIR)
        hot = hot_ref[q_rows, q0 : q0 + QCOLS, :].reshape(QB, PAIR)
        crops = jnp.where(lanes_of(hot) < 4, (hot.astype(f32) - 1.0) * BIG, 0.0).astype(bf16)
        sides = stacked(*(jnp.concatenate([own_lanes(queries, head, 0.125), crops], axis=1) for head in range(2)))
        keys = jnp.concatenate([window(keys_ref, i, c0, width), window(hot_ref, i, c0, width)], axis=1)
        size = keys.shape[0] - HALF * width
        return dot_nt(keys[:size], sides[:LATE]), dot_nt(keys, sides[LATE:])

    def attend(i, j, *scores):
        q0, c0, width = COLS[j]
        q_rows = query_rows(i)
        values_t = window(values_ref, i, c0, width).T
        values_t = jnp.concatenate([values_t, jnp.ones((16, values_t.shape[1]), bf16)], axis=0)
        bias = bias_ref[:, (0 if j != 0 else 16) : (64 if j != 2 else 48), :].reshape(HALF * width, LATE)
        half = LATE // 2
        outs, rates = [], []
        for k, part in enumerate(scores):
            above = part.shape[0] - HALF * width
            own = part[above:] + bias
            part = jnp.concatenate([part[:above], own], axis=0) if above else own
            chances = powers(part, jnp.max(part, axis=0, keepdims=True))
            ref, at = ((early_ref, AT_EARLY), (late_ref, AT_LATE))[k]
            put_tiles(ref.at[i // 2, lax.rem(i, 2)], at[j], chances)
            summed = dot(values_t[:, : chances.shape[0]], chances)
            rates.append(1.0 / summed[PAIR : PAIR + 1])
            summed = summed[:PAIR] * rates[k]
            outs.append(jnp.concatenate([summed[:HD, :half], summed[HD:, half:]], axis=0).T)
        rate_ref[i * 3 + j, 0:1] = jnp.concatenate(rates, axis=1)
        both = jnp.concatenate(outs, axis=0).astype(bf16)
        att_ref[q_rows, q0 : q0 + QCOLS, :] = both.reshape(QROWS, QCOLS, PAIR)

    def block_row(i, ready, following):
        for j in range(3):
            now = ready
            if j < 2:
                ready = score(i, j + 1)
            else:
                for ref, value in zip(ready_refs, score(following, 0)):
                    ref[...] = value
            attend(i, j, *now)

    def move(half, start):
        for copy in copies(half):
            copy.start() if start else copy.wait()

    @pl.when(pair > 0)
    def _():
        move(0, False)

    block_row(0, score(0, 0), 1)

    @pl.loop(1, CROWS // QROWS)
    def _(i):
        @pl.when((i == 2) & (pair > 0))
        def _():
            move(1, False)

        block_row(i, [ref[...] for ref in ready_refs], jnp.minimum(i + 1, CROWS // QROWS - 1))

        @pl.when(i == 1)
        def _():
            move(0, True)

        if talks:

            @pl.when((i == 2) & (pair == pairs - 1))
            def _():
                weights.first(REDUCE).wait()
                weights.second(REDUCE).start()

    move(1, True)

    @pl.when(pair == pairs - 1)
    def _():
        for half in range(2):
            for copy in copies(half):
                copy.wait()

    if talks:

        @pl.when(pair == 0)
        def _():
            weights.first(HEADS).wait()
            weights.second(HEADS).start()
            for name in (MERGE, EXPAND, REDUCE):
                weights.first(name).start()

        @pl.when(pair == 1)
        def _():
            weights.first(QV).wait()
            weights.first(HIDDEN).wait()
            weights.second(HEADS).wait()

        @pl.when(pair == 2)
        def _():
            for name in (MERGE, EXPAND):
                weights.first(name).wait()
                weights.second(name).start()

        @pl.when(pair == pairs - 1)
        def _():
            for k in range(HEADS + 1):
                got[k][...] = landing[k][...]
            for name in (MERGE, EXPAND, REDUCE):
                weights.second(name).wait()


def column_blocks():
    return [
        pl.BlockSpec((CROWS, CCOLS, PAIR), functools.partial(lambda at, g: (0, 0, at), k), pipeline_mode=pl.Buffered(1))
        for k in range(D // PAIR)
    ]


def attend_forward(x, w, biases, hot, others, talks):
    pairs = D // PAIR
    anywhere = pl.BlockSpec(memory_space=pl.ANY)

    def held(*shape):
        return pl.BlockSpec(shape, lambda g: (0,) * len(shape), pipeline_mode=pl.Buffered(1))

    shape = jax.ShapeDtypeStruct
    if talks:
        got = [shape(array.shape, array.dtype) for array in (biases, others[0], w, *others[1:])]
        small = got[: HEADS + 1]
        got_specs = [held(*array.shape) for array in small] + [anywhere] * (len(others) - 1)
        other_specs = [held(*others[0].shape)] + [anywhere] * (len(others) - 1)
        landing = [pltpu.VMEM(array.shape, array.dtype) for array in small]
        talk = [pltpu.SemaphoreType.DMA((12,)), pltpu.SemaphoreType.DMA((12,))]
        params = pltpu.CompilerParams(vmem_limit_bytes=56 * MIB, collective_id=1, has_side_effects=True)
    else:
        got, got_specs, landing, talk = [], [], [], []
        other_specs = [held(*array.shape) for array in others]
        params = pltpu.CompilerParams(vmem_limit_bytes=56 * MIB)
    return pl.pallas_call(
        functools.partial(attend_forward_kernel, talks),
        grid=(pairs,),
        in_specs=[column_blocks(), held(*w.shape), held(*biases.shape), held(CROWS, CCOLS, PAIR), other_specs],
        out_specs=[
            pl.BlockSpec((2, 3, CROWS, CCOLS, PAIR), lambda g: (g // 2, 0, 0, 0, 0)),
            pl.BlockSpec((CROWS, CCOLS, PAIR), lambda g: (0, 0, g)),
            pl.BlockSpec((None, 12, 8, 2 * LATE), lambda g: (g, 0, 0, 0)),
            anywhere,
            anywhere,
            got_specs,
        ],
        out_shape=[
            shape((pairs, 3, CROWS, CCOLS, PAIR), bf16),
            shape((CROWS, CCOLS, pairs * PAIR), bf16),
            shape((pairs, 12, 8, 2 * LATE), f32),
            shape((pairs, CROWS // QROWS, LATE // PAIR, ROWS_EARLY, PAIR), bf16),
            shape((pairs, CROWS // QROWS, LATE // PAIR, ROWS_LATE, PAIR), bf16),
            got,
        ],
        scratch_shapes=[
            pltpu.VMEM((HALF, 2 * QCOLS, LATE), f32),
            pltpu.VMEM(w.shape, bf16),
            pltpu.VMEM(biases.shape, f32),
            pltpu.VMEM((2, 2, LATE // PAIR, ROWS_EARLY, PAIR), bf16),
            pltpu.VMEM((2, 2, LATE // PAIR, ROWS_LATE, PAIR), bf16),
            pltpu.VMEM((12 * COLS[0][2], LATE), f32),
            pltpu.VMEM((16 * COLS[0][2], LATE), f32),
            pltpu.SemaphoreType.DMA((2, 2)),
            landing,
            talk,
        ],
        compiler_params=params,
        cost_estimate=pl.CostEstimate(flops=24_000_000_000, bytes_accessed=60 * MIB, transcendentals=16_000_000),
        name="attend_forward",
    )([x] * (D // PAIR), w, biases, hot, others)


class Links:
    def __init__(self, send, recv):
        self.me, self.place = lax.axis_index("dp"), lax.axis_index("mp")
        self.send, self.recv, self.used = send, recv, 0

    def across(self):
        return self.me, 1 - self.place

    def numbers(self, count):
        self.used += count
        return self.used - count

    def copy(self, source, target, number, to):
        return pltpu.make_async_remote_copy(
            src_ref=source,
            dst_ref=target,
            send_sem=self.send.at[number],
            recv_sem=self.recv.at[number],
            device_id=to,
            device_id_type=pl.DeviceIdType.MESH,
        )

    def meet(self, others):
        barrier = pltpu.get_barrier_semaphore()
        for other in others:
            pl.semaphore_signal(barrier, inc=1, device_id=other, device_id_type=pl.DeviceIdType.MESH)
        pl.semaphore_wait(barrier, len(others))


class Levels:
    def __init__(self, links, groups):
        self.links, self.groups = links, groups

    def __len__(self):
        return len(self.groups)

    def parts(self, level):
        return 1 << len(self.groups[level])

    def index(self, device, level):
        return lax.rem(device // (1 << self.groups[level][0]), self.parts(level))

    def near(self, level):
        me, found = self.links.me, []
        for k in range(1, self.parts(level)):
            to = me
            for n, b in enumerate(self.groups[level]):
                if k >> n & 1:
                    to = to + (1 << b) * (1 - 2 * lax.rem(me // (1 << b), 2))
            found.append((k - 1, (to, self.links.place)))
        return found

    def owned(self, rows, level):
        start, size = 0, rows
        for k in range(level):
            size //= self.parts(k)
            start = start + self.index(self.links.me, k) * size
        return start, size

    def shares(self, rows, level):
        start, size = self.owned(rows, level)
        size //= self.parts(level)
        away = [start + self.index(to, level) * size for _, (to, _) in self.near(level)]
        return start + self.index(self.links.me, level) * size, away, size


def rows_at(ref, start, size):
    return ref.at[pl.ds(pl.multiple_of(start, 16), size)]


def add_rows(target, first, others, step):
    @pl.loop(0, target.shape[0] // step)
    def _(k):
        rows = pl.ds(pl.multiple_of(k * step, 16), step)
        total = first[rows].astype(f32)
        for other in others:
            total = total + other[rows].astype(f32)
        target[rows] = total.astype(target.dtype)


def add_small(running, arrived):
    terms = [running[...]] + arrived
    while len(terms) > 1:
        terms = [terms[k] + terms[k + 1] for k in range(0, len(terms), 2)]
    running[...] = terms[0]


class FeedSum:
    def __init__(self, links, levels, before, own, other, work, work_other, full, parts, parts_other, part_cross, tiny=None):
        self.links, self.levels, self.before = links, levels, before
        self.sources, self.works, self.full = (own, other), (work, work_other), full
        self.parts, self.part_cross = (parts, parts_other), part_cross
        self.rows = work.shape[0]
        self.tiny = tiny
        downs = [("down", level) for level in range(len(levels))]
        ups = [("up", level) for level in reversed(range(len(levels)))]
        self.stages = downs[:before] + [("cross", 0)] + downs[before:] + ups
        self.last = len(self.stages)
        self.base = [links.numbers(3 * levels.parts(level)) for _, level in self.stages]

    def copies(self, stage):
        links, levels, base = self.links, self.levels, self.base[stage]
        kind, level = self.stages[stage]
        near = levels.near(level)
        if kind == "up":
            mine = rows_at(self.full, *levels.owned(self.rows, level + 1))
            return [links.copy(mine, mine, base + k, to) for k, to in near]
        if kind == "cross":
            near = [(0, links.across())]
            kept = rows_at(self.works[1], *levels.owned(self.rows, self.before))
            made = [links.copy(kept, self.part_cross, base, links.across())]
        else:
            made = self.shared(stage, 1 if level < self.before else 0)
        if self.tiny:
            number = base + 2 * levels.parts(level)
            _, running, arrived = self.tiny
            made += [links.copy(running, arrived.at[stage, k], number + k, to) for k, to in near]
        return made

    def shared(self, stage, side):
        levels, base, level = self.levels, self.base[stage], self.stages[stage][1]
        _, away, size = levels.shares(self.rows, level)
        source = self.sources[side] if level == 0 else self.works[side]
        made = []
        for k, to in levels.near(level):
            number, part = base + side * levels.parts(level) + k, self.parts[side][level].at[k]
            made.append(self.links.copy(rows_at(source, away[k], size), part, number, to))
        return made

    def gather(self, stage, side):
        levels, level = self.levels, self.stages[stage][1]
        kept, _, size = levels.shares(self.rows, level)
        source = rows_at(self.sources[side] if level == 0 else self.works[side], kept, size)
        target = rows_at(self.full if level == len(levels) - 1 else self.works[side], kept, size)
        parts = [self.parts[side][level].at[k] for k, _ in levels.near(level)]
        add_rows(target, source, parts, levels.owned(self.rows, len(levels))[1])

    def finish(self, stage):
        levels = self.levels
        kind, level = self.stages[stage]
        for copy in self.copies(stage):
            copy.wait()
        unit = levels.owned(self.rows, len(levels))[1]
        if kind == "cross":
            mine = rows_at(self.works[0], *levels.owned(self.rows, self.before))
            add_rows(mine, mine, [self.part_cross], unit)
        elif kind == "down":
            self.gather(stage, 1 if level < self.before else 0)
        if self.tiny and kind != "up":
            _, running, arrived = self.tiny
            if kind == "cross":
                running[0:8] += arrived[stage, 0, 0:8]
                running[8:10] += arrived[stage, 0, 10:12]
            else:
                add_small(running, [arrived[stage, k] for k, _ in levels.near(level)])

    def step(self, stage):
        if 2 <= stage <= self.before + 1:
            for copy in self.shared(stage - 2, 0):
                copy.wait()
            self.gather(stage - 2, 0)
        if stage > 0:
            self.finish(stage - 1)
        elif self.tiny:
            self.tiny[1][...] = self.tiny[0][...]
        if stage < self.last:
            for copy in self.copies(stage):
                copy.start()
        if 1 <= stage <= self.before:
            for copy in self.shared(stage - 1, 0):
                copy.start()


class HeadSum:
    def __init__(self, links, levels, away, arrived, work, full, parts, bias_away, bias_arrived, bias, bias_parts):
        self.links, self.levels = links, levels
        self.away, self.arrived, self.work, self.full, self.parts = away, arrived, work, full, parts
        self.bias_away, self.bias_arrived, self.bias, self.bias_parts = bias_away, bias_arrived, bias, bias_parts
        self.rows = work.shape[0]
        self.cross_base = links.numbers(2)
        self.last = 2 * len(levels)
        self.base = [links.numbers(2 * levels.parts(self.level(stage))) for stage in range(self.last)]

    def level(self, stage):
        return min(stage, self.last - 1 - stage)

    def cross(self):
        to = self.links.across()
        return [
            self.links.copy(self.away, self.arrived, self.cross_base, to),
            self.links.copy(self.bias_away, self.bias_arrived, self.cross_base + 1, to),
        ]

    def arriving(self, level, k):
        first, size = 0, self.rows
        for at in range(level):
            size //= self.levels.parts(at)
            first += size * (self.levels.parts(at) - 1)
        size //= self.levels.parts(level)
        return self.parts.at[first + k * size : first + (k + 1) * size]

    def copies(self, stage):
        links, levels, base, level = self.links, self.levels, self.base[stage], self.level(stage)
        near = levels.near(level)
        if stage >= len(levels):
            mine = rows_at(self.full, *levels.owned(self.rows, level + 1))
            return [links.copy(mine, mine, base + k, to) for k, to in near]
        _, away, size = levels.shares(self.rows, level)
        return [
            links.copy(rows_at(self.work, away[k], size), self.arriving(level, k), base + k, to) for k, to in near
        ] + [links.copy(self.bias, self.bias_parts.at[level, k], base + levels.parts(level) + k, to) for k, to in near]

    def step(self, stage):
        levels = self.levels
        unit = levels.owned(self.rows, len(levels))[1]
        for copy in self.cross() if stage == 0 else self.copies(stage - 1):
            copy.wait()
        if stage == 0:
            add_rows(self.work, self.work, [self.arrived], unit)
            self.bias[...] += self.bias_arrived[...]
        elif stage <= len(levels):
            level = stage - 1
            kept, _, size = levels.shares(self.rows, level)
            source = rows_at(self.work, kept, size)
            target = rows_at(self.full, kept, size) if stage == len(levels) else source
            add_rows(target, source, [self.arriving(level, k) for k, _ in levels.near(level)], unit)
            add_small(self.bias, [self.bias_parts[level, k] for k, _ in levels.near(level)])
        if stage < self.last:
            for copy in self.copies(stage):
                copy.start()


def groups_of(dp):
    bits = list(range(dp.bit_length() - 1))
    return [bits[:1], bits[1:2], bits[2:]], [bits[:1], bits[1:]]


PLAN = {
    (0, 1): [("expand", 1), ("reduce", 1)],
    (1, 2): [("reduce", 2), ("expand", 2)],
    (1, 4): [("reduce", 3), (0, "cross")],
    (2, 0): [("expand", 3)],
    (2, 1): [(1, "cross")],
    (2, 2): [("reduce", 4)],
    (2, 3): [("expand", 4)],
    (2, 4): [(0, 0)],
    (3, 0): [("reduce", 5)],
    (3, 1): [(0, 1)],
    (3, 2): [("expand", 5)],
    (3, 3): [("reduce", 6), (0, 2)],
    (3, 4): [(1, 0)],
    (4, 1): [(1, 1), ("expand", 6), ("reduce", 7)],
    (4, 2): [(0, 3)],
    (4, 3): [(1, 2), ("expand", 7)],
    (4, 4): [(0, 4), (1, 3), (1, 4)],
}


def attend_backward_kernel(
    dp, qkv_ref, go_ref, delta_ref, rate_ref, x_hbm, w_hbms, gone_hbm, early_hbm, late_hbm, feeds, merges, tiny_ref,
    gx_hbm, gw_ref, gb_ref, sums_out, gk_ref, gv_ref, gqkv_all, early_ref, late_ref, gx_ref, x_ref, w_ref, sems, talk,
):
    pairs = pl.num_programs(0) - 1
    step = pl.program_id(0)
    pair = lax.rem(step + pairs // 2, pairs)
    if dp:
        expand_out, reduce_out, merge_out, small_out, hidden_out = sums_out
        turned_ref, *talk = talk
        expand, reduce, heads, (small, small_in), (send, recv) = talk
        links = Links(send, recv)
        feed_levels, pair_levels = (Levels(links, groups) for groups in groups_of(dp))
        sums = {
            "expand": FeedSum(links, feed_levels, 1, *feeds[0], *expand, tiny=(tiny_ref, small, small_in)),
            "reduce": FeedSum(links, feed_levels, 2, *feeds[1], *reduce),
        }
        for number in range(2):
            sums[number] = HeadSum(links, pair_levels, *heads[number])

    def act(what, stage):
        if stage == "cross":
            for copy in sums[what].cross():
                copy.start()
        else:
            sums[what].step(stage)
            if what == "expand" and stage == sums[what].last:
                leave["expand"].start()
                small_out[...] = small[0:8]
                hidden_out[...] = jnp.concatenate([small[8:9], small[9:10]], axis=1)
            if what == "reduce" and stage == sums[what].last:
                for at in range(0, FF // 2, D):
                    turned_ref[at : at + D] = sums[what].full[:, at : at + D].T
                leave["reduce"].start()

    def event(at_step, place):
        if not dp or (at_step, place) not in PLAN:
            return

        @pl.when(step == at_step)
        def _():
            for what, stage in PLAN[at_step, place]:
                act(what, stage)

    def stored(of, half):
        rows = pl.ds(2 * half, 2)
        return [
            pltpu.make_async_copy(early_hbm.at[of, rows], early_ref.at[half], sems.at[half, 0]),
            pltpu.make_async_copy(late_hbm.at[of, rows], late_ref.at[half], sems.at[half, 1]),
        ]

    fill = pltpu.make_async_copy(gone_hbm, gx_ref, sems.at[2, 0])
    x_in = [
        pltpu.make_async_copy(x_hbm.at[:, :, pl.ds(k * PAIR, PAIR)], x_ref.at[k], sems.at[3 + k, 0])
        for k in range(D // PAIR)
    ]
    w_in = [pltpu.make_async_copy(w_hbms[k], w_ref.at[k], sems.at[3 + k, 1]) for k in range(2)]
    gx_out = [
        pltpu.make_async_copy(gx_ref.at[pl.ds(k * 8, 8)], gx_hbm.at[pl.ds(k * 8, 8)], sems.at[7 + k, 0])
        for k in range(4)
    ]
    if dp:
        leave = {
            "expand": pltpu.make_async_copy(sums["expand"].full, expand_out, sems.at[7, 1]),
            "reduce": pltpu.make_async_copy(turned_ref, reduce_out, sems.at[8, 1]),
        }

    @pl.when(step == 0)
    def _():
        for copy in [*stored(pair, 0), *x_in, *w_in, fill]:
            copy.start()
        if dp:
            links.meet([links.across()] + [to for level in range(2) for _, to in pair_levels.near(level)])
            for name in ("expand", "reduce"):
                sums[name].step(0)

    def fetch(half):
        if half == 0:
            for copy in stored(pair, 1):
                copy.start()
        else:

            @pl.when(step < pairs - 1)
            def _():
                for copy in stored(lax.rem(step + 1 + pairs // 2, pairs), 0):
                    copy.start()

        for copy in stored(pair, half):
            copy.wait()

    @pl.when(step < pairs)
    def _():
        attend_backward_pair(
            pair, qkv_ref, go_ref, delta_ref, rate_ref, gqkv_all.at[pair], early_ref, late_ref, gk_ref, gv_ref, fetch,
            lambda slot: [event(k, slot) for k in range(4)],
        )
        grad = jnp.concatenate([gqkv_all[pair, part].reshape(POS, PAIR) for part in range(3)], axis=1)

        @pl.when(step == 0)
        def _():
            for copy in x_in:
                copy.wait()

        x_all = jnp.concatenate([x_ref[k].reshape(POS, PAIR) for k in range(D // PAIR)], axis=1)
        grad_weights = dot_tn(grad, x_all).T.astype(bf16)
        grad_bias = jnp.broadcast_to(jnp.sum(grad.astype(f32), axis=0, keepdims=True), (8, 3 * PAIR))
        if not dp:
            gw_ref[...] = grad_weights
            gb_ref[...] = grad_bias
        else:
            for number in range(2):
                one = sums[number]
                for first, ref, small_ref in ((0, one.away, one.bias_away), (2, one.work, one.bias)):

                    @pl.when(step == first + number)
                    def _():
                        ref[:, 0 : 3 * PAIR] = grad_weights
                        small_ref[...] = grad_bias
                        if number == 0:
                            merge = merges[1 if first == 0 else 0]
                            for k in range(2):
                                span = slice(k * (D // 2), (k + 1) * (D // 2))
                                ref[span, 3 * PAIR :] = merge[:, span]

            for k in range(4):
                event(k, 4)

    @pl.when(step == pairs)
    def _():
        for copy in [fill, *w_in]:
            copy.wait()
        weights = jnp.concatenate(
            [
                w_ref[p // 2, part, :, p % 2 * PAIR : (p % 2 + 1) * PAIR]
                for p in range(D // PAIR)
                for part in range(3)
            ],
            axis=1,
        )
        for part in range(4):
            event(4, part)
            rows = slice(part * 8, part * 8 + 8)
            grads = [gqkv_all[p, k, rows].reshape(8 * CCOLS, PAIR) for p in range(D // PAIR) for k in range(3)]
            product = dot_nt(jnp.concatenate(grads, axis=1), weights).reshape(8, CCOLS, D)
            gx_ref[rows] = (gx_ref[rows].astype(f32) + product).astype(bf16)
            gx_out[part].start()
        event(4, 4)
        if dp:
            for number in range(2):
                for part in range(3):
                    lanes = slice(part * PAIR, (part + 1) * PAIR)
                    gw_ref[part, :, number * PAIR : (number + 1) * PAIR] = sums[number].full[:, lanes]
            for k in range(2):
                span = slice(k * (D // 2), (k + 1) * (D // 2))
                merge_out[:, span] = sums[0].full[span, 3 * PAIR :]
            for row, part in enumerate((0, 2)):
                lanes = slice(part * PAIR, (part + 1) * PAIR)
                gb_ref[row : row + 1] = jnp.concatenate([sums[p].bias[0:1, lanes] for p in range(2)], axis=1)
            for copy in leave.values():
                copy.wait()
        for copy in gx_out:
            copy.wait()


def attend_backward_pair(
    pair, qkv_ref, go_ref, delta_ref, rate_ref, gqkv_ref, early_ref, late_ref, gk_ref, gv_ref, fetch, event
):
    gk_ref[...] = jnp.zeros_like(gk_ref)
    gv_ref[...] = jnp.zeros_like(gv_ref)

    def gap(i, j):
        q0, c0, width = COLS[j]
        q_rows = query_rows(i)
        grads = go_ref[q_rows, q0 : q0 + QCOLS, :].reshape(QB, PAIR)
        deltas = delta_ref[q_rows, q0 : q0 + QCOLS, :].reshape(QB, PAIR)
        values = window(qkv_ref.at[2], i, c0, width)
        ones = jnp.broadcast_to(lane_row(0, 24), values.shape)
        values = jnp.concatenate([values, ones], axis=1)
        size = values.shape[0] - HALF * width
        own_grad = stacked(*(own_lanes(grads, head) for head in range(2)))
        own_delta = stacked(*(deltas * lane_row(3 * (2 * pair + head), 3) for head in range(2)))
        sides = jnp.concatenate([own_grad, own_delta], axis=1)
        return dot_nt(values[:size], sides[:LATE]), dot_nt(values, sides[LATE:]), own_grad

    def block(i, j, gaps, gaps_late, own_grad):
        q0, c0, width = COLS[j]
        q_rows = query_rows(i)
        queries = qkv_ref[0, q_rows, q0 : q0 + QCOLS, :].reshape(QB, PAIR)
        own = stacked(*(own_lanes(queries, head, 0.125) for head in range(2)))
        keys = window(qkv_ref.at[1], i, c0, width)
        count = keys.shape[0]
        size = count - HALF * width
        rate = rate_ref[i * 3 + j, 0:1, :].astype(bf16)
        chances = get_tiles(early_ref.at[i // 2, i % 2], AT_EARLY[j], size) * rate[:, :LATE]
        late = get_tiles(late_ref.at[i // 2, i % 2], AT_LATE[j], count) * rate[:, LATE:]
        slopes = chances * gaps.astype(bf16)
        slopes_late = late * gaps_late.astype(bf16)
        both = jnp.concatenate([slopes, slopes_late[:size]], axis=1)
        out = dot_tn(both, keys[:size])
        out_late = out[LATE:] + dot_tn(slopes_late[size:], keys[size:])
        half = LATE // 2
        out = [jnp.where(lanes_of(part[:half]) < HD, part[:half], part[half:]) for part in (out[:LATE], out_late)]
        out = (jnp.concatenate(out, axis=0) * 0.125).astype(bf16)
        gqkv_ref[0, q_rows, q0 : q0 + QCOLS, :] = out.reshape(QROWS, QCOLS, PAIR)
        rows = key_rows(i)
        for ref, early, later, side in ((gk_ref, slopes, slopes_late, own), (gv_ref, chances, late, own_grad)):
            both = jnp.concatenate([early, later[:size]], axis=1)
            part = jnp.concatenate([dot(both, side), dot(later[size:], side[LATE:])], axis=0)
            ref[rows, c0 : c0 + width, :] += part.reshape(-1, width, PAIR)

    order = [(i, j) for i in range(CROWS // QROWS) for j in range(3)]
    ready = gap(*order[0])
    for n, (i, j) in enumerate(order):
        now = ready
        if n + 1 < len(order):
            ready = gap(*order[n + 1])
        if j == 0 and i % 2 == 0:
            fetch(i // 2)
        block(i, j, *now)
        if j == 2:
            event(i)

    gqkv_ref[1] = gk_ref[...].astype(bf16)
    gqkv_ref[2] = gv_ref[...].astype(bf16)


def attend_backward(qkv, grad_att, delta, rate, x, w_halves, grad_one, a_stored, b_stored, feeds, merges, tiny, dp):
    pairs = D // PAIR
    levels, pair_levels = ([1 << len(group) for group in groups] for groups in groups_of(max(dp, 1)))

    def turn(g):
        return lax.rem(jnp.minimum(g, pairs - 1) + pairs // 2, pairs)

    def held(*shape):
        return pl.BlockSpec(shape, lambda g: (0,) * len(shape), pipeline_mode=pl.Buffered(1))

    shape, vmem = jax.ShapeDtypeStruct, pltpu.VMEM
    anywhere = pl.BlockSpec(memory_space=pl.ANY)
    outs = [((CROWS, CCOLS, D), bf16)]
    if dp:
        wide = FF // 2
        feed_specs, merge_specs, tiny_spec = [[held(D, wide)] * 2] * 2, [held(D // 2, D)] * 2, held(16, D)
        sum_outs = [((D, wide), bf16), ((wide, D), bf16), ((D // 2, D), bf16), ((8, D), f32), ((1, wide), f32)]
        sum_specs = [anywhere, anywhere] + [held(*dims) for dims, _ in sum_outs[2:]]
        outs += [((3, D, 2 * PAIR), bf16), ((2, 2 * PAIR), f32)]
        out_specs = [anywhere] + [held(*dims) for dims, _ in outs[1:]]
        copies = 2 * 3 * (2 * sum(levels) + max(levels)) + 2 * (2 + 4 * sum(pair_levels))

        def feed_scratch(before):
            parts, size = [], D
            for level in levels:
                size //= level
                parts.append(vmem((level - 1, size, wide), bf16))
            crossing = D
            for level in levels[:before]:
                crossing //= level
            return [vmem((D, wide), bf16)] * 3 + [parts, parts[:before], vmem((crossing, wide), bf16)]

        talk = [
            vmem((wide, D), bf16),
            feed_scratch(1),
            feed_scratch(2),
            [
                [vmem((D, width), bf16)] * 5
                + [vmem((8, 3 * PAIR), f32)] * 3
                + [vmem((len(pair_levels), max(pair_levels) - 1, 8, 3 * PAIR), f32)]
                for width in (3 * PAIR + D // 2, 3 * PAIR)
            ],
            [vmem((16, D), f32), vmem((len(levels) + 1, max(levels) - 1, 16, D), f32)],
            [pltpu.SemaphoreType.DMA((copies,)), pltpu.SemaphoreType.DMA((copies,))],
        ]
        params = pltpu.CompilerParams(vmem_limit_bytes=63 * MIB, collective_id=0, has_side_effects=True)
    else:
        feeds, merges, tiny, feed_specs, merge_specs, tiny_spec, sum_outs, sum_specs, talk = ([] for _ in range(9))
        outs += [((pairs, D, 3 * PAIR), bf16), ((pairs, 8, 3 * PAIR), f32)]
        out_specs = [
            anywhere,
            pl.BlockSpec((None, D, 3 * PAIR), lambda g: (turn(g), 0, 0)),
            pl.BlockSpec((None, 8, 3 * PAIR), lambda g: (turn(g), 0, 0)),
        ]
        params = pltpu.CompilerParams(vmem_limit_bytes=60 * MIB)
    return pl.pallas_call(
        functools.partial(attend_backward_kernel, dp),
        grid=(pairs + 1,),
        in_specs=[
            pl.BlockSpec((None, 3, CROWS, CCOLS, PAIR), lambda g: (turn(g), 0, 0, 0, 0)),
            pl.BlockSpec((CROWS, CCOLS, PAIR), lambda g: (0, 0, turn(g))),
            held(CROWS, CCOLS, PAIR),
            pl.BlockSpec((None, 12, 8, 2 * LATE), lambda g: (turn(g), 0, 0, 0)),
            anywhere,
            [anywhere] * 2,
            anywhere, anywhere, anywhere,
            feed_specs,
            merge_specs,
            tiny_spec,
        ],
        out_specs=[*out_specs, sum_specs],
        out_shape=[shape(*out) for out in outs] + [[shape(*out) for out in sum_outs]],
        scratch_shapes=[
            vmem((CROWS, CCOLS, PAIR), f32),
            vmem((CROWS, CCOLS, PAIR), f32),
            vmem((pairs, 3, CROWS, CCOLS, PAIR), bf16),
            vmem((2, 2, LATE // PAIR, ROWS_EARLY, PAIR), bf16),
            vmem((2, 2, LATE // PAIR, ROWS_LATE, PAIR), bf16),
            vmem((CROWS, CCOLS, D), bf16),
            vmem((D // PAIR, CROWS, CCOLS, PAIR), bf16),
            vmem((2, 3, D, 2 * PAIR), bf16),
            pltpu.SemaphoreType.DMA((11, 2)),
            talk,
        ],
        compiler_params=params,
        cost_estimate=pl.CostEstimate(flops=50_000_000_000, bytes_accessed=90 * MIB, transcendentals=0),
        name="attend_backward",
    )(qkv, grad_att, delta, rate, x, w_halves, grad_one, a_stored, b_stored, feeds, merges, tiny)


ROWS = 512
CHUNK = 512


def feed_kernel(
    x_ref, ct_ref, att_ref, wm_refs, we_refs, be_refs, wr_refs, vec_refs,
    out_ref, gone_ref, gatt_ref, delta_ref, expand_refs, reduce_refs, merge_refs, tiny_ref,
    hid_ref, slope_ref, gpre_ref, grad_rows_t, acc_m, acc_e, acc_r, acc_be, acc_vec, choose_ref, kind_ref,
):
    step = pl.program_id(0)
    last = pl.num_programs(0) - 1
    slot = lax.rem(step, 2)

    @pl.when(step == 0)
    def _():
        for ref in (hid_ref, grad_rows_t, acc_m, acc_e, acc_r, acc_be, acc_vec):
            ref[...] = jnp.zeros_like(ref)
        lane = lax.broadcasted_iota(jnp.int32, (D, PAIR), 1)
        head = lax.broadcasted_iota(jnp.int32, (D, PAIR), 0) // HD
        choose_ref[...] = jnp.where(head == lane // 3, -1.0, 0.0).astype(bf16)
        kind_ref[...] = jnp.where(lane[0:8] % 3 == lax.broadcasted_iota(jnp.int32, (8, PAIR), 0), 1.0, 0.0)

    b_merge, gain_one, shift_one, b_reduce, gain_two, shift_two = (ref[...] for ref in vec_refs)
    half = D // 2
    chunks = [(side, at) for side in range(2) for at in range(0, FF // 2, CHUNK)]
    spans = [slice(n * CHUNK, (n + 1) * CHUNK) for n in range(len(chunks))]

    def normal(z):
        centred = z - jnp.mean(z, axis=1, keepdims=True)
        rate = lax.rsqrt(jnp.mean(centred * centred, axis=1, keepdims=True) + 1e-5)
        return centred * rate, rate

    def normal_back(grad, normed, rate):
        mean = jnp.mean(grad, axis=1, keepdims=True)
        slant = jnp.mean(grad * normed, axis=1, keepdims=True)
        return rate * (grad - mean - normed * slant)

    def column_sum(z):
        return jnp.sum(z, axis=0, keepdims=True)

    def eights(z):
        return sum(z[at : at + 8] for at in range(0, z.shape[0], 8))


    def weight_reduce(n):
        acc_r[:, spans[n]] += dot(grad_rows_t[...], hid_ref[1 - slot, :, spans[n]])

    def norm_one(x, branch):
        first, rate = normal(x.astype(f32) + b_merge + branch)
        normed = first * gain_one + shift_one
        return first, rate, normed, normed.astype(bf16)

    def norm_two(z, cotangent):
        second, rate = normal(z)
        cotangent = cotangent.astype(f32)
        grad = normal_back(cotangent * gain_two, second, rate)
        out = (second * gain_two + shift_two).astype(bf16)
        return out, grad, grad.astype(bf16), eights(cotangent * second), eights(cotangent), eights(grad)

    def back_one(grad_normed, first, rate):
        grad = normal_back(grad_normed * gain_one, first, rate)
        return grad.astype(bf16), eights(grad_normed * first), eights(grad_normed), eights(grad)

    def gelu(pre):
        square = pre * pre
        bent = jnp.tanh(pre * (GC + (GC * GA) * square))
        lead = 0.5 + 0.5 * bent
        hidden = pre * lead
        slope = lead + (hidden * (1.0 - bent)) * (GC + (3 * GC * GA) * square)
        return hidden.astype(bf16), slope.astype(bf16)

    def back(grad, slope):
        grad = (grad * slope.astype(f32)).astype(bf16)
        return grad, eights(grad.astype(f32))

    def expand(rows_in, n):
        side, at = chunks[n]
        return dot(rows_in, we_refs[side][:, at : at + CHUNK]) + be_refs[side][0:1, at : at + CHUNK]

    def grad_hidden(grad_rows, n):
        side, at = chunks[n]
        return dot_nt(grad_rows, wr_refs[side][at : at + CHUNK, :])

    @pl.when(step == last)
    def _():
        for n in range(len(chunks)):
            weight_reduce(n)
        for side in range(2):
            span = slice(side * (FF // 2), (side + 1) * (FF // 2))
            expand_refs[side][...] = acc_e[:, span].astype(bf16)
            reduce_refs[side][...] = acc_r[:, span].astype(bf16)
            merge_refs[side][...] = acc_m[side * half : (side + 1) * half].astype(bf16)
        tiny_ref[...] = jnp.zeros_like(tiny_ref)
        tiny_ref[0:8] = acc_vec[...]
        for k in range(FF // D):
            tiny_ref[8 + k : 9 + k] = acc_be[:, k * D : (k + 1) * D]

    @pl.when(step < last)
    def _():
        branch_one = dot(att_ref[:, :half], wm_refs[0][...]) + dot(att_ref[:, half:], wm_refs[1][...])
        for n in range(len(chunks) // 2):
            weight_reduce(n)
        first, rate_one, normed_one, rows_in = sliced(norm_one, 32, x_ref[...], branch_one)
        summed_two = normed_one + b_reduce
        ready = expand(rows_in, 0)
        for n, (side, at) in enumerate(chunks):
            now = ready
            if n + 1 < len(chunks):
                ready = expand(rows_in, n + 1)
            hidden, slope = sliced(gelu, 16, now)
            hid_ref[slot, :, spans[n]] = hidden
            slope_ref[:, spans[n]] = slope
            summed_two += dot(hidden, wr_refs[side][at : at + CHUNK, :])
        for n in range(len(chunks) // 2, len(chunks)):
            weight_reduce(n)
        out_ref[...], grad_two, grad_rows, *partial = sliced(norm_two, 32, summed_two, ct_ref[...])
        for k, part in zip((4, 5, 3), partial):
            acc_vec[k : k + 1] += column_sum(part)
        grad_rows_t[...] = grad_rows.T
        grad_normed = grad_two
        ready = grad_hidden(grad_rows, 0)
        for n, (side, at) in enumerate(chunks):
            now = ready
            if n + 1 < len(chunks):
                ready = grad_hidden(grad_rows, n + 1)
            grad_pre, part = sliced(back, 32, now, slope_ref[:, spans[n]])
            gpre_ref[:, spans[n]] = grad_pre
            acc_be[:, spans[n]] += column_sum(part)
            grad_normed += dot_nt(grad_pre, we_refs[side][:, at : at + CHUNK])
        rows_t = rows_in.T
        for n in range(len(chunks)):
            acc_e[:, spans[n]] += dot(rows_t, gpre_ref[:, spans[n]])
        grad_one_rows, *partial = sliced(back_one, 32, grad_normed, first, rate_one)
        gone_ref[...] = grad_one_rows
        for k, part in zip((1, 2, 0), partial):
            acc_vec[k : k + 1] += column_sum(part)
        for side in range(2):
            gatt_ref[:, side * half : (side + 1) * half] = dot_nt(grad_one_rows, wm_refs[side][...]).astype(bf16)
        acc_m[...] += dot(att_ref[...].T, grad_one_rows)
        products = gatt_ref[...].astype(f32) * att_ref[...].astype(f32)
        deltas = three_parts(dot(products.astype(bf16), choose_ref[...]))
        delta_ref[...] = sum(part * kind_ref[k : k + 1] for k, part in enumerate(deltas)).astype(bf16)


def feed(x, cotangent, att, wms, wes, be, wrs, vecs):
    half = D // 2

    def rows(width):
        return pl.BlockSpec((ROWS, width), lambda s: (jnp.minimum(s, POS // ROWS - 1), 0))

    def whole(*shape):
        return pl.BlockSpec(shape, lambda s: (0, 0), pipeline_mode=pl.Buffered(1))

    def held(*shape):
        return pl.BlockSpec(shape, lambda s: (0, 0))

    shape = jax.ShapeDtypeStruct
    return pl.pallas_call(
        feed_kernel,
        grid=(POS // ROWS + 1,),
        in_specs=[
            rows(D), rows(D), rows(D), [whole(half, D)] * 2, [whole(D, FF // 2)] * 2,
            [whole(1, FF // 2)] * 2, [whole(FF // 2, D)] * 2, [whole(1, D)] * 6,
        ],
        out_specs=[
            rows(D), rows(D), rows(D), rows(PAIR), [held(D, FF // 2)] * 2, [held(D, FF // 2)] * 2, [held(half, D)] * 2,
            held(16, D),
        ],
        out_shape=[
            shape((POS, D), bf16), shape((POS, D), bf16), shape((POS, D), bf16), shape((POS, PAIR), bf16),
            [shape((D, FF // 2), bf16)] * 2, [shape((D, FF // 2), bf16)] * 2, [shape((half, D), bf16)] * 2,
            shape((16, D), f32),
        ],
        scratch_shapes=[
            pltpu.VMEM((2, ROWS, FF), bf16),
            pltpu.VMEM((ROWS, FF), bf16),
            pltpu.VMEM((ROWS, FF), bf16),
            pltpu.VMEM((D, ROWS), bf16),
            pltpu.VMEM((D, D), f32),
            pltpu.VMEM((D, FF), f32),
            pltpu.VMEM((D, FF), f32),
            pltpu.VMEM((1, FF), f32),
            pltpu.VMEM((8, D), f32),
            pltpu.VMEM((D, PAIR), bf16),
            pltpu.VMEM((8, PAIR), f32),
        ],
        compiler_params=pltpu.CompilerParams(vmem_limit_bytes=60 * MIB),
        cost_estimate=pl.CostEstimate(flops=44_000_000_000, bytes_accessed=40 * MIB, transcendentals=6_000_000),
        name="feed",
    )(x, cotangent, att, wms, wes, be, wrs, vecs)


def finish_kernel(*refs):
    count = (len(refs) - 5) // 2
    for source, target in zip(refs[: count - 1], refs[count:-6]):
        target[...] = source[...].astype(f32)
    for k, target in enumerate(refs[-6:]):
        target[...] = refs[count - 1][k : k + 1]


def finish(wide, small, vecs):
    def block(array, parts):
        dims = array.shape
        part = dims[:-2] + (dims[-2] // parts, dims[-1])
        return pl.BlockSpec(part, lambda s: (0,) * (len(dims) - 2) + ((s if parts > 1 else 0), 0))

    parts = 2
    specs = [block(array, parts) for array in wide] + [block(array, 1) for array in small]
    row = jax.ShapeDtypeStruct((1, D), f32)
    return pl.pallas_call(
        finish_kernel,
        grid=(parts,),
        in_specs=specs + [block(vecs, 1)],
        out_specs=specs + [block(row, 1)] * 6,
        out_shape=[jax.ShapeDtypeStruct(array.shape, f32) for array in (*wide, *small)] + [row] * 6,
        compiler_params=pltpu.CompilerParams(vmem_limit_bytes=63 * MIB),
        cost_estimate=pl.CostEstimate(flops=0, bytes_accessed=20 * MIB, transcendentals=0),
        name="finish",
    )(*wide, *small, vecs)


def local(
    inputs, crop_ids, w_heads, b_heads, w_merge, b_merge, gain_one, shift_one, w_expand, b_expand, w_reduce,
    b_reduce, gain_two, shift_two, cotangent, *, split,
):
    features = inputs.shape[2]
    dp, mp = split
    paired = mp == 2
    talks = paired and dp >= 8 and dp & (dp - 1) == 0 and D % (16 * dp) == 0
    place = lax.axis_index("mp")

    def both(shard, axis):
        if paired:
            return [shard, lax.ppermute(shard, "mp", [(0, 1), (1, 0)])]
        whole = lax.all_gather(shard, "mp", axis=axis, tiled=True)
        return list(jnp.split(whole, 2, axis=axis))

    def sum_parts(parts, axis):
        if paired:
            arrived = lax.ppermute(parts[1], "mp", [(0, 1), (1, 0)])
            return parts[0].astype(f32) + arrived.astype(f32)
        return lax.psum_scatter(jnp.concatenate(parts, axis=axis), "mp", scatter_dimension=axis, tiled=True)

    canvas = inputs[0].reshape(CROWS, CCOLS, features)
    labels = lax.dynamic_index_in_dim(crop_ids, place, 0, keepdims=False)
    hot = (labels[:, None] == jnp.arange(PAIR)[None, :]).astype(bf16).reshape(CROWS, CCOLS, PAIR)

    own_heads = jnp.transpose(w_heads, (1, 0, 2))
    vecs = [vec[None] for vec in (b_merge, gain_one, shift_one, b_reduce, gain_two, shift_two)]

    if talks:
        qkv, att, rate, a_stored, b_stored, got = attend_forward(
            canvas, own_heads, b_heads, hot, [b_expand[None], w_merge, w_expand, w_reduce], True
        )
        heads, merges = [own_heads, got[HEADS]], [w_merge, got[MERGE]]
        expands, reduces = [w_expand, got[EXPAND]], [w_reduce, got[REDUCE]]
        hiddens = [b_expand[None], got[HIDDEN]]
    else:
        heads, merges, expands, reduces = both(own_heads, 2), both(w_merge, 0), both(w_expand, 1), both(w_reduce, 0)
        biases = [part.astype(f32) for part in both(b_heads.astype(bf16), 1)]
        hiddens = [part[None].astype(f32) for part in both(b_expand.astype(bf16), 0)]
        qkv, att, rate, a_stored, b_stored, _ = attend_forward(
            canvas, heads[0], biases[0], hot, [heads[1], biases[1]], False
        )
    outputs, grad_one, grad_att, delta, expand_g, reduce_g, merge_g, tiny = feed(
        inputs[0], cotangent[0], att.reshape(POS, -1), merges, expands, hiddens, reduces, vecs
    )

    def canvas_of(array):
        return array.reshape(CROWS, CCOLS, -1)

    grad_inputs, heads_g, bias_g, sums = attend_backward(
        qkv, canvas_of(grad_att), canvas_of(delta), rate, canvas, heads, canvas_of(grad_one), a_stored, b_stored,
        [expand_g, reduce_g], merge_g, tiny, dp if talks else 0,
    )

    def bias_part(g_bias):
        g_bias = g_bias[:, 0].reshape(-1, 3, PAIR)
        return jnp.stack([g_bias[:, 0].reshape(-1), g_bias[:, 2].reshape(-1)])

    if talks:
        expand_g, reduce_g, merge_g, tiny_g, be_g = sums
        grad_inputs, expand_g, reduce_g, merge_g, heads_g, be_g, bias_g, *tiny_g = finish(
            [grad_inputs.reshape(POS, D), expand_g, reduce_g, merge_g, heads_g], [be_g, bias_g], tiny_g
        )
        be_g = be_g[0]
        tiny_g = [vec[0] for vec in tiny_g]
    else:
        heads_g = heads_g.reshape(-1, D, 3, PAIR).transpose(2, 1, 0, 3).reshape(3, D, -1)
        grads = (
            (jnp.split(heads_g, 2, axis=2), 2),
            (jnp.split(bias_part(bias_g).astype(bf16), 2, axis=1), 1),
            (expand_g, 1),
            ([half.T for half in reduce_g], 0),
            (merge_g, 0),
            (jnp.split(tiny[8:12].reshape(-1).astype(bf16), 2), 0),
        )
        heads_g, bias_g, expand_g, reduce_g, merge_g, be_g = (
            lax.psum(sum_parts(list(parts), axis).astype(bf16), "dp").astype(f32) for parts, axis in grads
        )
        tiny_g = lax.psum(tiny, ("dp", "mp"))
    return (
        outputs[None],
        grad_inputs.reshape(1, POS, D).astype(f32),
        jnp.transpose(heads_g.astype(f32), (1, 0, 2)),
        bias_g,
        merge_g.astype(f32),
        tiny_g[0],
        tiny_g[1],
        tiny_g[2],
        expand_g.astype(f32),
        be_g,
        reduce_g.astype(f32),
        tiny_g[3],
        tiny_g[4],
        tiny_g[5],
    )


def solution(mesh):
    rows = P(("dp", "mp"), None, None)
    weights = (P(None, None, "mp"), P(None, "mp"), P("mp", None))
    feeds = (P(None, "mp"), P("mp"), P("mp", None))
    return jax.shard_map(
        functools.partial(local, split=(mesh.shape["dp"], mesh.shape["mp"])),
        mesh=mesh,
        in_specs=(rows, P("dp", None), *weights, P(), P(), P(), *feeds, P(), P(), P(), rows),
        out_specs=(rows, rows, *weights, P(), P(), P(), *feeds, P(), P(), P()),
        check_vma=False,
    )
```

time: 5470 us -> 224 us (0.04)
  local copies, waits for them, and re-layouts: 4280 us -> 0.85 us
  matrix products: 488 us -> 0 us
  other arithmetic: 463 us -> 1.3 us
  Pallas kernels: 0 us -> 220 us
  blocking collectives: 101 us -> 0 us
  waiting for transfers between devices: 77.5 us -> 0 us
    scatter-add x96 -> x0, local copies, waits for them, and re-layouts: 3320 us -> none  [unmemory(): canvas_grid.at[row_at:row_at + 2 * QROWS, col_at:col_at + 2 * QCOLS]]
    dot_general x40 -> x0, matrix products: 488 us -> none  [the longest x4 69.5 us: attend_backward(): jnp.einsum('bqhe,bkhe->bhqk', grad_blocks, value_blocks, preferred_elemen...]
    reshape x334 -> x0, local copies, waits for them, and re-layouts: 355 us -> none  [the longest x288 292 us: memory(): return jnp.stack(pieces)]
    pallas_call x0 -> x4, Pallas kernels: none -> 220 us  [the longest x1 97.4 us: attend_backward(): pl.pallas_call(functools.partial(attend_backward_kernel, dp), grid=(pairs...]
    add x72 -> x0, other arithmetic: 179 us -> none  [unmemory(): canvas_grid.at[row_at:row_at + 2 * QROWS, col_at:col_at + 2 * QCOLS]]
    while x560 -> x0, local copies, waits for them, and re-layouts: 175 us -> none
    another operation x121 -> x0, local copies, waits for them, and re-layouts: 134 us -> none
    slice x57 -> x0, local copies, waits for them, and re-layouts: 100 us -> none  [the longest x24 54.7 us: memory(): portion = canvas_grid[row_at:row_at + 2 * QROWS, col_at:col_at + 2 * QCOLS]]
  transfers between devices with their start and end apart: 9 -> 0, of which waited for: 4 -> 0; matrix products, arithmetic and copies ran while one was open for 94% -> 0% of each run, Pallas kernels for 0% -> 0%
where the time goes in v1:
time: 224 us; the launch traced here: 223 us
  Pallas kernels  220 us (98%)
    pallas_call x1, Pallas kernels, attend_backward(): pl.pallas_call(functools.partial(attend_backward_kernel, dp), grid=(pairs...  97.4 us
    pallas_call x1, Pallas kernels, feed(): pl.pallas_call(feed_kernel, grid=(POS // ROWS + 1,), in_specs=[rows(D), r...  65.6 us
    pallas_call x1, Pallas kernels, attend_forward(): pl.pallas_call(functools.partial(attend_forward_kernel, talks), grid=(pai...  50.7 us
    pallas_call x1, Pallas kernels, finish(): pl.pallas_call(finish_kernel, grid=(parts,), in_specs=specs + [block(vecs...  6.67 us

profile of v1, /device:TPU:0, one launch (start us, length us, event | category | flops | bytes accessed | tf_op | source)
XLA Modules:
  0.0 223.4 jit_solution(3327786687232561784)
XLA Ops:
  0.6 0.0 copy-start
  0.7 0.7 copy-done
  1.4 0.1 eq.16
  1.5 1.3 fusion.hot_ref
  2.8 50.7 %attend_forward.1 = (bf16[4,3,32,96,128]{4,3,2,1,0:T(8,128)(2,1)}, bf16[32,96,512]{2,1,0:T(8,128)(2,1)}, f32[4,12,8,512]{3,2,1,0:T(8,128)}, bf16[4,4,2,1920,128]...) custom-call(bf16[32,96,512]{2,1,0:T(8,128)(2,1)} %bitcast.29, ...), custom_call_target="tpu_custom_call" | custom-call | flops 24000000000 | bytes 62914560 | tf_op jit(solution)/shard_map/attend_forward/pallas_call | solution.py:354
  53.5 65.6 %feed.1 = (bf16[3072,512]{1,0:T(8,128)(2,1)}, bf16[3072,512]{1,0:T(8,128)(2,1)}, bf16[3072,512]{1,0:T(8,128)(2,1)}, bf16[3072,128]{1,0:T(8,128)(2,1)}, bf16[512,...) custom-call(bf16[3072,512]{1,0:T(8,128)(2,1)} %bitcast.33, ...), custom_call_target="tpu_custom_call" | custom-call | flops 44000002048 | bytes 41943040 | tf_op jit(solution)/shard_map/feed/pallas_call | solution.py:1123
  119.2 97.4 %attend_backward.1 = (bf16[32,96,512]{2,1,0:T(8,128)(2,1)}, bf16[3,512,256]{2,1,0:T(8,128)(2,1)}, f32[2,256]{1,0:T(2,128)}, bf16[512,1024]{1,0:T(8,128)(2,1)}, b...) custom-call(bf16[4,3,32,96,128]{4,3,2,1,0:T(8,128)(2,1)} %get-tuple-element.62.qkv_re, ...), custom_call_target="tpu_custom_call" | custom-call | flops 49999998976 | bytes 94371840 | tf_op jit(solution)/shard_map/attend_backward/pallas_call | solution.py:931
  216.5 0.0 copy-start.1
  216.5 6.7 %finish.1 = (f32[3072,512]{1,0:T(8,128)}, f32[512,1024]{1,0:T(8,128)}, f32[1024,512]{1,0:T(8,128)}, f32[256,512]{1,0:T(8,128)}, f32[3,512,256]{2,1,0:T(8,128)}, ...) custom-call(bf16[3072,512]{1,0:T(8,128)(2,1)} %bitcast.26, ...), custom_call_target="tpu_custom_call" | custom-call | bytes 20971520 | tf_op jit(solution)/shard_map/finish/pallas_call | solution.py:1175
  223.2 0.0 copy-done.1
  (1 shorter events, 0.0 us)
Async XLA Ops:
  0.6 0.7 copy-start
  216.5 6.7 %copy-start.1 = (s32[2,3072]{1,0:T(2,128)S(1)}, s32[2,3072]{1,0:T(2,128)}, u32[]{:S(2)}) copy-start(s32[2,3072]{1,0:T(2,128)} %param.16) | copy-start | bytes 73732

commit v2 on v1

--- a/solution.py
+++ b/solution.py
@@ -477,9 +477,9 @@
 
 
 class FeedSum:
-    def __init__(self, links, levels, before, own, other, work, work_other, full, parts, parts_other, part_cross, tiny=None):
+    def __init__(self, links, levels, before, work, work_other, full, parts, parts_other, part_cross, tiny=None):
         self.links, self.levels, self.before = links, levels, before
-        self.sources, self.works, self.full = (own, other), (work, work_other), full
+        self.works, self.full = (work, work_other), full
         self.parts, self.part_cross = (parts, parts_other), part_cross
         self.rows = work.shape[0]
         self.tiny = tiny
@@ -511,7 +511,7 @@
     def shared(self, stage, side):
         levels, base, level = self.levels, self.base[stage], self.stages[stage][1]
         _, away, size = levels.shares(self.rows, level)
-        source = self.sources[side] if level == 0 else self.works[side]
+        source = self.works[side]
         made = []
         for k, to in levels.near(level):
             number, part = base + side * levels.parts(level) + k, self.parts[side][level].at[k]
@@ -521,7 +521,7 @@
     def gather(self, stage, side):
         levels, level = self.levels, self.stages[stage][1]
         kept, _, size = levels.shares(self.rows, level)
-        source = rows_at(self.sources[side] if level == 0 else self.works[side], kept, size)
+        source = rows_at(self.works[side], kept, size)
         target = rows_at(self.full if level == len(levels) - 1 else self.works[side], kept, size)
         parts = [self.parts[side][level].at[k] for k, _ in levels.near(level)]
         add_rows(target, source, parts, levels.owned(self.rows, len(levels))[1])
@@ -628,19 +628,17 @@
 
 PLAN = {
     (0, 1): [("expand", 1), ("reduce", 1)],
-    (1, 2): [("reduce", 2), ("expand", 2)],
-    (1, 4): [("reduce", 3), (0, "cross")],
-    (2, 0): [("expand", 3)],
-    (2, 1): [(1, "cross")],
-    (2, 2): [("reduce", 4)],
+    (1, 1): [("reduce", 2), ("expand", 2)],
+    (1, 3): [("reduce", 3)],
+    (1, 4): [("expand", 3), (0, "cross")],
+    (2, 1): [("reduce", 4), (1, "cross")],
     (2, 3): [("expand", 4)],
-    (2, 4): [(0, 0)],
-    (3, 0): [("reduce", 5)],
+    (2, 4): [(0, 0), ("reduce", 5)],
     (3, 1): [(0, 1)],
-    (3, 2): [("expand", 5)],
-    (3, 3): [("reduce", 6), (0, 2)],
-    (3, 4): [(1, 0)],
-    (4, 1): [(1, 1), ("expand", 6), ("reduce", 7)],
+    (3, 2): [("expand", 5), ("reduce", 6)],
+    (3, 3): [(0, 2)],
+    (3, 4): [(1, 0), ("reduce", 7)],
+    (4, 1): [(1, 1), ("expand", 6)],
     (4, 2): [(0, 3)],
     (4, 3): [(1, 2), ("expand", 7)],
     (4, 4): [(0, 4), (1, 3), (1, 4)],
@@ -661,8 +659,8 @@
         links = Links(send, recv)
         feed_levels, pair_levels = (Levels(links, groups) for groups in groups_of(dp))
         sums = {
-            "expand": FeedSum(links, feed_levels, 1, *feeds[0], *expand, tiny=(tiny_ref, small, small_in)),
-            "reduce": FeedSum(links, feed_levels, 2, *feeds[1], *reduce),
+            "expand": FeedSum(links, feed_levels, 1, *expand, tiny=(tiny_ref, small, small_in)),
+            "reduce": FeedSum(links, feed_levels, 2, *reduce),
         }
         for number in range(2):
             sums[number] = HeadSum(links, pair_levels, *heads[number])
@@ -709,6 +707,11 @@
         for k in range(4)
     ]
     if dp:
+        feeds_in = [
+            pltpu.make_async_copy(feeds[n][side], sums[name].works[side], sems.at[11 + n, side])
+            for n, name in enumerate(("expand", "reduce"))
+            for side in range(2)
+        ]
         leave = {
             "expand": pltpu.make_async_copy(sums["expand"].full, expand_out, sems.at[7, 1]),
             "reduce": pltpu.make_async_copy(turned_ref, reduce_out, sems.at[8, 1]),
@@ -716,10 +719,14 @@
 
     @pl.when(step == 0)
     def _():
-        for copy in [*stored(pair, 0), *x_in, *w_in, fill]:
+        for copy in stored(pair, 0):
             copy.start()
         if dp:
+            for copy in feeds_in:
+                copy.start()
             links.meet([links.across()] + [to for level in range(2) for _, to in pair_levels.near(level)])
+            for copy in feeds_in:
+                copy.wait()
             for name in ("expand", "reduce"):
                 sums[name].step(0)
 
@@ -736,6 +743,11 @@
 
         for copy in stored(pair, half):
             copy.wait()
+
+        @pl.when(step == half)
+        def _():
+            for copy in [*w_in, fill] if half else x_in:
+                copy.start()
 
     @pl.when(step < pairs)
     def _():
@@ -888,7 +900,7 @@
     outs = [((CROWS, CCOLS, D), bf16)]
     if dp:
         wide = FF // 2
-        feed_specs, merge_specs, tiny_spec = [[held(D, wide)] * 2] * 2, [held(D // 2, D)] * 2, held(16, D)
+        feed_specs, merge_specs, tiny_spec = [[anywhere] * 2] * 2, [held(D // 2, D)] * 2, held(16, D)
         sum_outs = [((D, wide), bf16), ((wide, D), bf16), ((D // 2, D), bf16), ((8, D), f32), ((1, wide), f32)]
         sum_specs = [anywhere, anywhere] + [held(*dims) for dims, _ in sum_outs[2:]]
         outs += [((3, D, 2 * PAIR), bf16), ((2, 2 * PAIR), f32)]
@@ -954,7 +966,7 @@
             vmem((CROWS, CCOLS, D), bf16),
             vmem((D // PAIR, CROWS, CCOLS, PAIR), bf16),
             vmem((2, 3, D, 2 * PAIR), bf16),
-            pltpu.SemaphoreType.DMA((11, 2)),
+            pltpu.SemaphoreType.DMA((13, 2)),
             talk,
         ],
         compiler_params=params,

time: 224 us -> 222 us (level)
  no operation moved by 1% of the time
where the time goes in v2:
time: 222 us
  Pallas kernels  219 us (99%)
    pallas_call x1, Pallas kernels, attend_backward(): pl.pallas_call(functools.partial(attend_backward_kernel, dp), grid=(pairs...  95.8 us
    pallas_call x1, Pallas kernels, feed(): pl.pallas_call(feed_kernel, grid=(POS // ROWS + 1,), in_specs=[rows(D), r...  65.6 us
    pallas_call x1, Pallas kernels, attend_forward(): pl.pallas_call(functools.partial(attend_forward_kernel, talks), grid=(pai...  50.7 us
    pallas_call x1, Pallas kernels, finish(): pl.pallas_call(finish_kernel, grid=(parts,), in_specs=specs + [block(vecs...  6.67 us

profile of v2, /device:TPU:0, one launch (start us, length us, event | category | flops | bytes accessed | tf_op | source)
XLA Modules:
  0.0 221.9 jit_solution(7119706555427276551)
XLA Ops:
  0.6 0.0 copy-start
  0.7 0.7 copy-done
  1.4 0.1 eq.16
  1.5 1.3 fusion.hot_ref
  2.8 50.7 %attend_forward.1 = (bf16[4,3,32,96,128]{4,3,2,1,0:T(8,128)(2,1)}, bf16[32,96,512]{2,1,0:T(8,128)(2,1)}, f32[4,12,8,512]{3,2,1,0:T(8,128)}, bf16[4,4,2,1920,128]...) custom-call(bf16[32,96,512]{2,1,0:T(8,128)(2,1)} %bitcast.29, ...), custom_call_target="tpu_custom_call" | custom-call | flops 24000000000 | bytes 62914560 | tf_op jit(solution)/shard_map/attend_forward/pallas_call | solution.py:354
  53.5 65.6 %feed.1 = (bf16[3072,512]{1,0:T(8,128)(2,1)}, bf16[3072,512]{1,0:T(8,128)(2,1)}, bf16[3072,512]{1,0:T(8,128)(2,1)}, bf16[3072,128]{1,0:T(8,128)(2,1)}, bf16[512,...) custom-call(bf16[3072,512]{1,0:T(8,128)(2,1)} %bitcast.33, ...), custom_call_target="tpu_custom_call" | custom-call | flops 44000002048 | bytes 41943040 | tf_op jit(solution)/shard_map/feed/pallas_call | solution.py:1135
  119.2 95.8 %attend_backward.1 = (bf16[32,96,512]{2,1,0:T(8,128)(2,1)}, bf16[3,512,256]{2,1,0:T(8,128)(2,1)}, f32[2,256]{1,0:T(2,128)}, bf16[512,1024]{1,0:T(8,128)(2,1)}, b...) custom-call(bf16[4,3,32,96,128]{4,3,2,1,0:T(8,128)(2,1)} %get-tuple-element.62.qkv_re, ...), custom_call_target="tpu_custom_call" | custom-call | flops 49999998976 | bytes 94371840 | tf_op jit(solution)/shard_map/attend_backward/pallas_call | solution.py:943
  215.0 0.0 copy-start.1
  215.0 6.7 %finish.1 = (f32[3072,512]{1,0:T(8,128)}, f32[512,1024]{1,0:T(8,128)}, f32[1024,512]{1,0:T(8,128)}, f32[256,512]{1,0:T(8,128)}, f32[3,512,256]{2,1,0:T(8,128)}, ...) custom-call(bf16[3072,512]{1,0:T(8,128)(2,1)} %bitcast.26, ...), custom_call_target="tpu_custom_call" | custom-call | bytes 20971520 | tf_op jit(solution)/shard_map/finish/pallas_call | solution.py:1187
  221.7 0.0 copy-done.1
  (1 shorter events, 0.0 us)
Async XLA Ops:
  0.6 0.7 copy-start
  215.0 6.7 %copy-start.1 = (s32[2,3072]{1,0:T(2,128)S(1)}, s32[2,3072]{1,0:T(2,128)}, u32[]{:S(2)}) copy-start(s32[2,3072]{1,0:T(2,128)} %param.16) | copy-start | bytes 73732
